TPU v7x, 32 devices: a whole 2x2x4 slice. The times are simulated.
32 devices in a mesh: seq: 16 (over z, y, x), tp: 2 (over core).
Axes of the slice: x: 2, y: 2, z: 4, core: 2. Of those that a mesh axis runs over, the one named last changes fastest.
Arguments:
- student: bfloat16 [4096, 2048], P('seq'), may hold values from -6 to 6
- projector: bfloat16 [2, 4224, 2048], P('tp', 'seq'), may hold values from -0.125 to 0.125
- teacher: bfloat16 [2, 4096, 8448], P(None, 'seq', 'tp'), may hold values from -6 to 6
- layer_index: int32 [4096], P('seq'), may hold values from 0 to 1
- valid_mask: int32 [4096], P('seq'), may hold values 0 or 1
Outputs:
- grad_student: bfloat16 [4096, 2048], P('seq', 'tp')
- token_loss: float32 [4096], P(('seq', 'tp'))
All inputs are finite; a program needn't handle non-finite values. No bound on the sum of `valid_mask` on one device may be relied on, other than what follows from the above.
Results may differ from a plain program's by a relative error of at most 0.0034.
Values may be sent and summed in bfloat16 or wider, within the bound.
A program may use at most 64 MiB of HBM per device.

v0:
```python
import jax
import jax.numpy as jnp
from jax import lax
from jax.sharding import PartitionSpec as P

HW = 8448


def body(student, projector, teacher, layer_index, valid_mask):
    rows_dev = student.shape[0]
    feat_dim = student.shape[1]
    chosen = teacher[0]
    chosen = jnp.where((layer_index == 1)[:, None], teacher[1], chosen)
    weight = valid_mask.astype(jnp.float32)[:, None]
    gathered = lax.all_gather(projector, "seq", axis=1, tiled=True)
    flat_rows = gathered.reshape(-1, feat_dim)
    predicted = lax.dot_general(
        student, flat_rows, (((1,), (1,)), ((), ())), preferred_element_type=jnp.float32
    )
    difference = predicted - chosen.astype(jnp.float32)
    masked_err = (weight * difference).astype(jnp.bfloat16)
    grad_term = jnp.dot(masked_err, flat_rows, preferred_element_type=jnp.float32)
    squares = jnp.sum(difference * difference, axis=1)
    summed, totals = (
        lax.psum_scatter(grad_term, "tp", scatter_dimension=1, tiled=True),
        lax.psum_scatter(squares, "tp", scatter_dimension=0, tiled=True),
    )
    tp_count = lax.axis_size("tp")
    share_rows = rows_dev // tp_count
    own_mask = lax.dynamic_slice_in_dim(
        valid_mask, lax.axis_index("tp") * share_rows, share_rows
    ).astype(jnp.float32)
    return (summed.astype(jnp.bfloat16), own_mask * totals / HW)


def solution(mesh):
    placed = (P("seq", None), P("tp", "seq", None), P(None, "seq", "tp"), P("seq"), P("seq"))
    return jax.shard_map(
        body,
        mesh=mesh,
        in_specs=placed,
        out_specs=(P("seq", "tp"), P(("seq", "tp"))),
        check_vma=False,
    )
```

profile of v0, /device:TPU:0, one launch (start us, length us, event | category | flops | bytes accessed | tf_op | source)
XLA Modules:
  0.0 260.1 jit_solution(11113816485252569042)
XLA Ops:
  7.2 0.0 copy-start
  7.2 0.0 all-gather.2.cloned.1.call-start
  7.2 0.7 all-gather.2.cloned.1.call-update
  7.9 0.0 reduce-scatter.2.cloned.1.call-start
  8.0 0.7 convert_element_type.15
  8.6 0.7 broadcast_compare_fusion
  9.3 200.8 %all-gather.2.cloned.1.call-done = bf16[1,4224,2048]{2,1,0:T(8,128)(2,1)} async-done(((bf16[1,264,2048]{2,1,0:T(8,128)(2,1)}), bf16[1,4224,2048]{2,1,0:T(8,128)(2,1)}) %all-gather.2.cloned.1.call-update) | async-done | bytes 17301520 | tf_op jit(solution)/shard_map/all_gather | solution.py:15
  210.2 0.0 copy-done
  210.2 19.6 %multiply_reduce_fusion = (f32[256]{0:T(256)S(1)}, f32[256,4224]{1,0:T(8,128)}) fusion(bf16[2,256,4224]{2,1,0:T(8,128)(2,1)} %param.7, pred[256]{0:T(512)(128)(4,1)S(1)} %broadcast_compare_fusion, bf16[256,2048]{1,0:T(8,128)(2,1)S(1)} %copy-done, bf16[1,4224,2048]{2,1,0:T(8,128)(2,1)} %all-gather.2.cloned.1.call-done), kind=kOutput, calls=%fused_computation.5 | convolution fusion | flops 4434591744 | bytes 27002112 | tf_op jit(solution)/shard_map/dot_general | solution.py:17
  229.8 0.0 copy-start.2
  229.8 0.0 copy-start.1
  229.8 13.4 %fusion = f32[256,2048]{1,0:T(8,128)} fusion(bf16[1,4224,2048]{2,1,0:T(8,128)(2,1)} %all-gather.2.cloned.1.call-done, f32[256,4224]{1,0:T(8,128)} %get-tuple-element.3, f32[256]{0:T(256)S(1)} %convert_element_type.15), kind=kOutput, calls=%fused_computation | convolution fusion | flops 4431347712 | bytes 23725056 | tf_op jit(solution)/shard_map/dot_general | solution.py:22
  243.2 0.0 reduce-scatter.2.cloned.1.call-update
  243.2 0.0 copy-done.2
  243.2 0.6 dynamic-slice
  244.5 2.5 all-reduce
  246.9 0.0 copy-done.1
  246.9 0.6 fusion.8
  247.5 3.6 %reduce-scatter.2.cloned.1.call-done = f32[256,1024]{1,0:T(8,128)} async-done(((f32[256,2048]{1,0:T(8,128)}), f32[256,1024]{1,0:T(8,128)}) %reduce-scatter.2.cloned.1.call-update) | async-done | bytes 1048592 | tf_op jit(solution)/shard_map/reduce_scatter | solution.py:25
  251.2 2.1 convert_element_type.18
Async XLA Ops:
  7.2 203.0 %copy-start = (bf16[256,2048]{1,0:T(8,128)(2,1)S(1)}, bf16[256,2048]{1,0:T(8,128)(2,1)}, u32[]{:S(2)}) copy-start(bf16[256,2048]{1,0:T(8,128)(2,1)} %param.5) | copy-start | bytes 3145732
  7.2 203.0 %all-gather.2.cloned.1.call-start = ((), (), s32[]{:S(2)}) async-start(), calls=%async_computation.1 | async-start | bytes 18382848 | tf_op jit(solution)/shard_map/all_gather | solution.py:15
  7.9 243.3 %reduce-scatter.2.cloned.1.call-start = ((), (), s32[]{:S(2)}) async-start(), calls=%async_computation.2 | async-start | bytes 3145728 | tf_op jit(solution)/shard_map/reduce_scatter | solution.py:25
  229.8 13.5 %copy-start.2 = (u32[32]{0:T(128)S(1)}, u32[32]{0:T(128)}, u32[]{:S(2)}) copy-start(u32[32]{0:T(128)} %constant.20) | copy-start | bytes 388
  229.8 17.2 %copy-start.1 = (s32[256]{0:T(256)S(1)}, s32[256]{0:T(256)}, u32[]{:S(2)}) copy-start(s32[256]{0:T(256)} %param.9) | copy-start | bytes 3076
Sparse Core Ops, SparseCore 0:
  10.8 199.3 all-gather.1
  243.3 7.7 reduce-scatter.1
where the time goes:
time: 260 us
  waiting for transfers between devices  205 us (79%)
  matrix products  33 us (13%)
  between operations  14.7 us (6%)
  other arithmetic  4.05 us (2%)
    all_gather x1, waiting for transfers between devices, body(): gathered = lax.all_gather(projector, 'seq', axis=1, tiled=True)  201 us
    dot_general x1, matrix products, body(): lax.dot_general(student, flat_rows, (((1,), (1,)), ((), ())), preferred_e...  19.6 us
    dot_general x1, matrix products, body(): jnp.dot(masked_err, flat_rows, preferred_element_type=jnp.float32)  13.4 us
  transfers between devices with their start and end apart: 2, of which 2 were waited for; matrix products, arithmetic and copies ran while one was open for 1% of the time, Pallas kernels for 0%

commit v1 on v0

--- a/solution.py
+++ b/solution.py
@@ -1,3 +1,4 @@
+import functools
 import jax
 import jax.numpy as jnp
 from jax import lax
@@ -6,13 +7,39 @@
 HW = 8448
 
 
+def refer_point(base_x, a_name):
+    taken_in = lax.axis_index(a_name)
+    tile_out = lax.axis_size(a_name)
+    value_now, block_now, v_now = (tile_out, taken_in, base_x.shape[1])
+    all_rows = tuple(((k0, (k0 + 1) % value_now) for k0 in range(value_now)))
+    k_now = jnp.zeros((*base_x.shape[:1], value_now * v_now, *base_x.shape[2:]), base_x.dtype)
+    k_now = lax.dynamic_update_slice_in_dim(k_now, base_x, block_now * v_now, axis=1)
+    outer = b_next = base_x
+    frames = tuple(((k0, (k0 - 1) % value_now) for k0 in range(value_now)))
+    h_now = value_now // 2
+    for u in range(1, h_now + 1):
+        outer = lax.ppermute(outer, axis_name=a_name, perm=all_rows)
+        k_now = lax.dynamic_update_slice_in_dim(
+            k_now, outer, (block_now - u) % value_now * v_now, axis=1
+        )
+        if u < value_now - h_now:
+            b_next = lax.ppermute(b_next, axis_name=a_name, perm=frames)
+            k_now = lax.dynamic_update_slice_in_dim(
+                k_now, b_next, (block_now + u) % value_now * v_now, axis=1
+            )
+    return k_now
+
+
+core_number = functools.partial(refer_point, a_name="seq")
+
+
 def body(student, projector, teacher, layer_index, valid_mask):
     rows_dev = student.shape[0]
     feat_dim = student.shape[1]
     chosen = teacher[0]
     chosen = jnp.where((layer_index == 1)[:, None], teacher[1], chosen)
     weight = valid_mask.astype(jnp.float32)[:, None]
-    gathered = lax.all_gather(projector, "seq", axis=1, tiled=True)
+    gathered = core_number(projector)
     flat_rows = gathered.reshape(-1, feat_dim)
     predicted = lax.dot_general(
         student, flat_rows, (((1,), (1,)), ((), ())), preferred_element_type=jnp.float32

time: 260 us -> 409 us (1.57)
  starting transfers between devices: 0.08 us -> 96.8 us
  local copies, waits for them, and re-layouts: 0.6 us -> 43.8 us
  waiting for transfers between devices: 205 us -> 228 us
  matrix products: 33 us -> 19.5 us
    ppermute x0 -> x15, waiting for transfers between devices: none -> 221 us  [the longest x8 167 us: refer_point(): outer = lax.ppermute(outer, axis_name=a_name, perm=all_rows)]
    all_gather x1 -> x0, waiting for transfers between devices: 201 us -> none  [body(): gathered = lax.all_gather(projector, 'seq', axis=1, tiled=True)]
    ppermute x0 -> x15, starting transfers between devices: none -> 96.8 us  [the longest x7 83.9 us: refer_point(): b_next = lax.ppermute(b_next, axis_name=a_name, perm=frames)]
    dynamic_update_slice x0 -> x16, local copies, waits for them, and re-layouts: none -> 26.5 us  [the longest x8 13.9 us: refer_point(): lax.dynamic_update_slice_in_dim(k_now, outer, (block_now - u) % value_now...]
    dot_general x1, matrix products: 19.6 us -> 9.33 us  [body(): lax.dot_general(student, flat_rows, (((1,), (1,)), ((), ())), preferred_e...]
    unnamed x7 -> x19, local copies, waits for them, and re-layouts: 0.6 us -> 7.17 us
    reshape x0 -> x1, local copies, waits for them, and re-layouts: none -> 6.18 us  [body(): flat_rows = gathered.reshape(-1, feat_dim)]
  transfers between devices with their start and end apart: 2 -> 16, of which waited for: 2 -> 9; matrix products, arithmetic and copies ran while one was open for 1% -> 11% of each run, Pallas kernels for 0% -> 0%
where the time goes in v1:
time: 409 us; the launch traced here: 408 us
  waiting for transfers between devices  228 us (56%)
  starting transfers between devices  96.8 us (24%)
  local copies, waits for them, and re-layouts  43.8 us (11%)
  matrix products  19.5 us (5%)
  between operations  14.8 us (4%)
    ppermute x8, waiting for transfers between devices, refer_point(): outer = lax.ppermute(outer, axis_name=a_name, perm=all_rows)  167 us
    ppermute x7, starting transfers between devices, refer_point(): b_next = lax.ppermute(b_next, axis_name=a_name, perm=frames)  83.9 us
    ppermute x7, waiting for transfers between devices, refer_point(): b_next = lax.ppermute(b_next, axis_name=a_name, perm=frames)  54.1 us
    dynamic_update_slice x8, local copies, waits for them, and re-layouts, refer_point(): lax.dynamic_update_slice_in_dim(k_now, outer, (block_now - u) % value_now...  13.9 us
    ppermute x8, starting transfers between devices, refer_point(): outer = lax.ppermute(outer, axis_name=a_name, perm=all_rows)  12.9 us
    dynamic_update_slice x7, local copies, waits for them, and re-layouts, refer_point(): lax.dynamic_update_slice_in_dim(k_now, b_next, (block_now + u) % value_no...  11.6 us
    dot_general x1, matrix products, body(): jnp.dot(masked_err, flat_rows, preferred_element_type=jnp.float32)  10.2 us
    dot_general x1, matrix products, body(): lax.dot_general(student, flat_rows, (((1,), (1,)), ((), ())), preferred_e...  9.33 us
  transfers between devices with their start and end apart: 16, of which 9 were waited for; matrix products, arithmetic and copies ran while one was open for 11% of the time, Pallas kernels for 0%

profile of v1, /device:TPU:0, one launch (start us, length us, event | category | flops | bytes accessed | tf_op | source)
XLA Modules:
  0.0 408.3 jit_solution(14181497634271834836)
XLA Ops:
  7.2 0.0 copy-start
  7.2 0.0 reduce-scatter.2.cloned.1.call-start
  7.2 3.0 collective-permute-start
  10.2 4.1 collective-permute-start.1
  14.3 42.5 %collective-permute-done = bf16[1,264,2048]{2,1,0:T(8,128)(2,1)S(1)} collective-permute-done((bf16[1,264,2048]{2,1,0:T(8,128)(2,1)}, bf16[1,264,2048]{2,1,0:T(8,128)(2,1)S(1)}, u32[]{:S(2)}, u32[]{:S(2)}) %collective-permute-start) | collective-permute-done | bytes 1081376 | tf_op jit(solution)/shard_map/ppermute | solution.py:21
  56.8 2.4 collective-permute-start.2
  59.2 0.0 collective-permute-done.1
  59.2 3.2 collective-permute-start.3
  62.5 42.3 %collective-permute-done.2 = bf16[1,264,2048]{2,1,0:T(8,128)(2,1)} collective-permute-done((bf16[1,264,2048]{2,1,0:T(8,128)(2,1)S(1)}, bf16[1,264,2048]{2,1,0:T(8,128)(2,1)}, u32[]{:S(2)}, u32[]{:S(2)}) %collective-permute-start.2) | collective-permute-done | bytes 1081376 | tf_op jit(solution)/shard_map/ppermute | solution.py:21
  104.7 2.6 collective-permute-start.4
  107.3 3.9 fusion.4
  111.3 0.0 collective-permute-done.3
  111.3 3.1 collective-permute-start.5
  114.3 6.2 %reshape.73 = bf16[4224,2048]{1,0:T(8,128)(2,1)} broadcast(bf16[]{:T(256)} %constant.114.clone.1), dimensions={} | broadcast | bytes 17301506 | tf_op jit(solution)/shard_map/reshape | solution.py:43
  120.5 0.0 copy-done.3
  120.5 1.1 bitcast_dynamic-update-slice_fusion.15
  121.6 30.6 %collective-permute-done.4 = bf16[1,264,2048]{2,1,0:T(8,128)(2,1)} collective-permute-done((bf16[1,264,2048]{2,1,0:T(8,128)(2,1)}, bf16[1,264,2048]{2,1,0:T(8,128)(2,1)}, u32[]{:S(2)}, u32[]{:S(2)}) %collective-permute-start.4) | collective-permute-done | bytes 1081376 | tf_op jit(solution)/shard_map/ppermute | solution.py:21
  152.2 2.5 collective-permute-start.6
  154.7 4.1 %copy.11 = bf16[1,256,4224]{1,2,0:T(8,128)(2,1)} copy(bf16[1,256,4224]{2,1,0:T(8,128)(2,1)} %get-tuple-element.2) | data formatting | bytes 4325376
  158.9 2.4 copy.12
  161.3 0.0 copy-done.5
  161.3 2.3 bitcast_dynamic-update-slice_fusion.14
  163.6 0.0 collective-permute-done.5
  163.6 3.2 collective-permute-start.7
  166.8 2.3 bitcast_dynamic-update-slice_fusion.13
  169.1 30.3 %collective-permute-done.6 = bf16[1,264,2048]{2,1,0:T(8,128)(2,1)} collective-permute-done((bf16[1,264,2048]{2,1,0:T(8,128)(2,1)}, bf16[1,264,2048]{2,1,0:T(8,128)(2,1)}, u32[]{:S(2)}, u32[]{:S(2)}) %collective-permute-start.6) | collective-permute-done | bytes 1081376 | tf_op jit(solution)/shard_map/ppermute | solution.py:21
  199.4 2.5 collective-permute-start.8
  201.9 2.4 bitcast_dynamic-update-slice_fusion.12
  204.3 2.4 bitcast_dynamic-update-slice_fusion.11
  206.7 0.0 collective-permute-done.7
  206.7 19.6 %collective-permute-start.9 = (bf16[1,264,2048]{2,1,0:T(8,128)(2,1)S(1)}, bf16[1,264,2048]{2,1,0:T(8,128)(2,1)S(1)}, u32[]{:S(2)}, u32[]{:S(2)}) collective-permute-start(bf16[1,264,2048]{2,1,0:T(8,128)(2,1)S(1)} %collective-permute-done.7), channel_id=1, source_target_pairs={{0,30},{2,0},{4,2},{6,4},{8,6},{10,8},{12,10},{14,12},{16,14},{18,... | collective-permute-start | bytes 3244040 | tf_op jit(solution)/shard_map/ppermute | solution.py:26
  226.3 2.3 bitcast_dynamic-update-slice_fusion.10
  228.6 0.0 collective-permute-done.8
  228.6 0.0 collective-permute-start.10
  228.6 2.3 bitcast_dynamic-update-slice_fusion.9
  230.9 2.3 bitcast_dynamic-update-slice_fusion.8
  233.3 16.8 %collective-permute-done.9 = bf16[1,264,2048]{2,1,0:T(8,128)(2,1)S(1)} collective-permute-done((bf16[1,264,2048]{2,1,0:T(8,128)(2,1)S(1)}, bf16[1,264,2048]{2,1,0:T(8,128)(2,1)S(1)}, u32[]{:S(2)}, u32[]{:S(2)}) %collective-permute-start.9) | collective-permute-done | bytes 1081376 | tf_op jit(solution)/shard_map/ppermute | solution.py:26
  250.1 25.0 %collective-permute-start.11 = (bf16[1,264,2048]{2,1,0:T(8,128)(2,1)S(1)}, bf16[1,264,2048]{2,1,0:T(8,128)(2,1)S(1)}, u32[]{:S(2)}, u32[]{:S(2)}) collective-permute-start(bf16[1,264,2048]{2,1,0:T(8,128)(2,1)S(1)} %collective-permute-done.9), channel_id=1, source_target_pairs={{0,30},{2,0},{4,2},{6,4},{8,6},{10,8},{12,10},{14,12},{16,14},{18,... | collective-permute-start | bytes 3244040 | tf_op jit(solution)/shard_map/ppermute | solution.py:26
  275.1 1.1 bitcast_dynamic-update-slice_fusion.7
  276.3 0.0 collective-permute-done.10
  276.3 0.0 collective-permute-start.12
  276.3 1.1 bitcast_dynamic-update-slice_fusion.6
  277.4 1.1 bitcast_dynamic-update-slice_fusion.5
  278.5 19.1 %collective-permute-done.11 = bf16[1,264,2048]{2,1,0:T(8,128)(2,1)S(1)} collective-permute-done((bf16[1,264,2048]{2,1,0:T(8,128)(2,1)S(1)}, bf16[1,264,2048]{2,1,0:T(8,128)(2,1)S(1)}, u32[]{:S(2)}, u32[]{:S(2)}) %collective-permute-start.11) | collective-permute-done | bytes 1081376 | tf_op jit(solution)/shard_map/ppermute | solution.py:26
  297.6 25.7 %collective-permute-start.13 = (bf16[1,264,2048]{2,1,0:T(8,128)(2,1)S(1)}, bf16[1,264,2048]{2,1,0:T(8,128)(2,1)S(1)}, u32[]{:S(2)}, u32[]{:S(2)}) collective-permute-start(bf16[1,264,2048]{2,1,0:T(8,128)(2,1)S(1)} %collective-permute-done.11), channel_id=1, source_target_pairs={{0,30},{2,0},{4,2},{6,4},{8,6},{10,8},{12,10},{14,12},{16,14},{18,... | collective-permute-start | bytes 3244040 | tf_op jit(solution)/shard_map/ppermute | solution.py:26
  323.2 1.1 bitcast_dynamic-update-slice_fusion.4
  324.3 0.0 collective-permute-done.12
  324.3 0.0 collective-permute-start.14
  324.4 1.1 bitcast_dynamic-update-slice_fusion.3
  325.4 1.1 bitcast_dynamic-update-slice_fusion.2
  326.6 18.2 %collective-permute-done.13 = bf16[1,264,2048]{2,1,0:T(8,128)(2,1)S(1)} collective-permute-done((bf16[1,264,2048]{2,1,0:T(8,128)(2,1)S(1)}, bf16[1,264,2048]{2,1,0:T(8,128)(2,1)S(1)}, u32[]{:S(2)}, u32[]{:S(2)}) %collective-permute-start.13) | collective-permute-done | bytes 1081376 | tf_op jit(solution)/shard_map/ppermute | solution.py:26
  344.8 1.2 bitcast_dynamic-update-slice_fusion.1
  346.0 21.6 %collective-permute-done.14 = bf16[1,264,2048]{2,1,0:T(8,128)(2,1)S(1)} collective-permute-done((bf16[1,264,2048]{2,1,0:T(8,128)(2,1)S(1)}, bf16[1,264,2048]{2,1,0:T(8,128)(2,1)S(1)}, u32[]{:S(2)}, u32[]{:S(2)}) %collective-permute-start.14) | collective-permute-done | bytes 1081376 | tf_op jit(solution)/shard_map/ppermute | solution.py:21
  367.6 1.1 bitcast_dynamic-update-slice_fusion
  368.8 0.0 copy-done
  368.8 9.3 %multiply_reduce_fusion = (f32[256]{0:T(256)S(1)}, f32[256,4224]{0,1:T(8,128)S(1)}) fusion(bf16[1,256,4224]{1,2,0:T(8,128)(2,1)S(1)} %copy-done.2, bf16[1,256,4224]{1,2,0:T(8,128)(2,1)S(1)} %copy-done.1, pred[256]{0:T(512)(128)(4,1)S(1)} %broadcast_compare_fusion, bf16[4224,2048]{1,0:T(8,128)(2,1)} %bitcast_dynamic-update-slice_fusion, ...), kind=kOutput, calls=%fused_computation.2 | convolution fusion | flops 4434591744 | bytes 27002112 | tf_op jit(solution)/shard_map/dot_general | solution.py:44
  378.1 0.0 copy-start.7
  378.1 10.2 %fusion.1 = f32[256,2048]{1,0:T(8,128)} fusion(bf16[4224,2048]{1,0:T(8,128)(2,1)} %bitcast_dynamic-update-slice_fusion, f32[256,4224]{0,1:T(8,128)S(1)} %get-tuple-element.5, f32[256]{0:T(256)S(1)} %convert_element_type.15), kind=kOutput, calls=%fused_computation.4 | convolution fusion | flops 4431347712 | bytes 23725056 | tf_op jit(solution)/shard_map/dot_general | solution.py:49
  388.3 0.0 reduce-scatter.2.cloned.1.call-update
  388.4 0.6 dynamic-slice
  389.6 2.5 all-reduce
  392.1 0.6 fusion.3
  392.7 6.7 %reduce-scatter.2.cloned.1.call-done = f32[256,1024]{1,0:T(8,128)} async-done(((f32[256,2048]{1,0:T(8,128)}), f32[256,1024]{1,0:T(8,128)}) %reduce-scatter.2.cloned.1.call-update) | async-done | bytes 1048592 | tf_op jit(solution)/shard_map/reduce_scatter | solution.py:52
  399.4 2.1 convert_element_type.18
  (13 shorter events, 0.0 us)
Async XLA Ops:
  7.2 361.6 %copy-start = (bf16[256,2048]{1,0:T(8,128)(2,1)S(1)}, bf16[256,2048]{1,0:T(8,128)(2,1)}, u32[]{:S(2)}) copy-start(bf16[256,2048]{1,0:T(8,128)(2,1)} %param.5) | copy-start | bytes 3145732
  7.2 392.2 %reduce-scatter.2.cloned.1.call-start = ((), (), s32[]{:S(2)}) async-start(), calls=%async_computation.1 | async-start | bytes 3145728 | tf_op jit(solution)/shard_map/reduce_scatter | solution.py:52
  7.2 49.6 %collective-permute-start = (bf16[1,264,2048]{2,1,0:T(8,128)(2,1)}, bf16[1,264,2048]{2,1,0:T(8,128)(2,1)S(1)}, u32[]{:S(2)}, u32[]{:S(2)}) collective-permute-start(bf16[1,264,2048]{2,1,0:T(8,128)(2,1)} %param.6), channel_id=1, source_target_pairs={{0,2},{2,4},{4,6},{6,8},{8,10},{10,12},{12,14},{14,16},{16,18},{18... | collective-permute-start | bytes 3244040 | tf_op jit(solution)/shard_map/ppermute | solution.py:21
  10.2 49.0 %collective-permute-start.1 = (bf16[1,264,2048]{2,1,0:T(8,128)(2,1)}, bf16[1,264,2048]{2,1,0:T(8,128)(2,1)}, u32[]{:S(2)}, u32[]{:S(2)}) collective-permute-start(bf16[1,264,2048]{2,1,0:T(8,128)(2,1)} %param.6), channel_id=1, source_target_pairs={{0,30},{2,0},{4,2},{6,4},{8,6},{10,8},{12,10},{14,12},{16,14},{18,... | collective-permute-start | bytes 3244040 | tf_op jit(solution)/shard_map/ppermute | solution.py:26
  56.8 47.9 %copy-start.4 = (bf16[1,264,2048]{2,1,0:T(8,128)(2,1)}, bf16[1,264,2048]{2,1,0:T(8,128)(2,1)S(1)}, u32[]{:S(2)}) copy-start(bf16[1,264,2048]{2,1,0:T(8,128)(2,1)S(1)} %collective-permute-done) | copy-start | bytes 3244036
  56.8 47.9 %collective-permute-start.2 = (bf16[1,264,2048]{2,1,0:T(8,128)(2,1)S(1)}, bf16[1,264,2048]{2,1,0:T(8,128)(2,1)}, u32[]{:S(2)}, u32[]{:S(2)}) collective-permute-start(bf16[1,264,2048]{2,1,0:T(8,128)(2,1)S(1)} %collective-permute-done), channel_id=1, source_target_pairs={{0,2},{2,4},{4,6},{6,8},{8,10},{10,12},{12,14},{14,16},{16,18},{18... | collective-permute-start | bytes 3244040 | tf_op jit(solution)/shard_map/ppermute | solution.py:21
  59.2 52.0 %collective-permute-start.3 = (bf16[1,264,2048]{2,1,0:T(8,128)(2,1)}, bf16[1,264,2048]{2,1,0:T(8,128)(2,1)}, u32[]{:S(2)}, u32[]{:S(2)}) collective-permute-start(bf16[1,264,2048]{2,1,0:T(8,128)(2,1)} %collective-permute-done.1), channel_id=1, source_target_pairs={{0,30},{2,0},{4,2},{6,4},{8,6},{10,8},{12,10},{14,12},{16,14},{18,... | collective-permute-start | bytes 3244040 | tf_op jit(solution)/shard_map/ppermute | solution.py:26
  104.7 47.5 %collective-permute-start.4 = (bf16[1,264,2048]{2,1,0:T(8,128)(2,1)}, bf16[1,264,2048]{2,1,0:T(8,128)(2,1)}, u32[]{:S(2)}, u32[]{:S(2)}) collective-permute-start(bf16[1,264,2048]{2,1,0:T(8,128)(2,1)} %collective-permute-done.2), channel_id=1, source_target_pairs={{0,2},{2,4},{4,6},{6,8},{8,10},{10,12},{12,14},{14,16},{16,18},{18... | collective-permute-start | bytes 3244040 | tf_op jit(solution)/shard_map/ppermute | solution.py:21
  111.2 9.3 %copy-start.3 = (bf16[1,264,2048]{2,1,0:T(8,128)(2,1)S(1)}, bf16[1,264,2048]{2,1,0:T(8,128)(2,1)}, u32[]{:S(2)}) copy-start(bf16[1,264,2048]{2,1,0:T(8,128)(2,1)} %param.6) | copy-start | bytes 3244036
  111.2 43.5 %copy-start.6 = (s32[256]{0:T(256)S(1)}, s32[256]{0:T(256)}, u32[]{:S(2)}) copy-start(s32[256]{0:T(256)} %param.8) | copy-start | bytes 3076
  111.3 52.4 %collective-permute-start.5 = (bf16[1,264,2048]{2,1,0:T(8,128)(2,1)}, bf16[1,264,2048]{2,1,0:T(8,128)(2,1)}, u32[]{:S(2)}, u32[]{:S(2)}) collective-permute-start(bf16[1,264,2048]{2,1,0:T(8,128)(2,1)} %collective-permute-done.3), channel_id=1, source_target_pairs={{0,30},{2,0},{4,2},{6,4},{8,6},{10,8},{12,10},{14,12},{16,14},{18,... | collective-permute-start | bytes 3244040 | tf_op jit(solution)/shard_map/ppermute | solution.py:26
  152.2 47.2 %collective-permute-start.6 = (bf16[1,264,2048]{2,1,0:T(8,128)(2,1)}, bf16[1,264,2048]{2,1,0:T(8,128)(2,1)}, u32[]{:S(2)}, u32[]{:S(2)}) collective-permute-start(bf16[1,264,2048]{2,1,0:T(8,128)(2,1)} %collective-permute-done.4), channel_id=1, source_target_pairs={{0,2},{2,4},{4,6},{6,8},{8,10},{10,12},{12,14},{14,16},{16,18},{18... | collective-permute-start | bytes 3244040 | tf_op jit(solution)/shard_map/ppermute | solution.py:21
  154.7 6.6 %copy-start.5 = (s32[256]{0:T(256)S(1)}, s32[256]{0:T(256)}, u32[]{:S(2)}) copy-start(s32[256]{0:T(256)} %param.9) | copy-start | bytes 3076
  163.6 43.0 %collective-permute-start.7 = (bf16[1,264,2048]{2,1,0:T(8,128)(2,1)}, bf16[1,264,2048]{2,1,0:T(8,128)(2,1)S(1)}, u32[]{:S(2)}, u32[]{:S(2)}) collective-permute-start(bf16[1,264,2048]{2,1,0:T(8,128)(2,1)} %collective-permute-done.5), channel_id=1, source_target_pairs={{0,30},{2,0},{4,2},{6,4},{8,6},{10,8},{12,10},{14,12},{16,14},{18,... | collective-permute-start | bytes 3244040 | tf_op jit(solution)/shard_map/ppermute | solution.py:26
  199.4 29.2 %collective-permute-start.8 = (bf16[1,264,2048]{2,1,0:T(8,128)(2,1)}, bf16[1,264,2048]{2,1,0:T(8,128)(2,1)S(1)}, u32[]{:S(2)}, u32[]{:S(2)}) collective-permute-start(bf16[1,264,2048]{2,1,0:T(8,128)(2,1)} %collective-permute-done.6), channel_id=1, source_target_pairs={{0,2},{2,4},{4,6},{6,8},{8,10},{10,12},{12,14},{14,16},{16,18},{18... | collective-permute-start | bytes 3244040 | tf_op jit(solution)/shard_map/ppermute | solution.py:21
  206.7 43.4 %collective-permute-start.9 = (bf16[1,264,2048]{2,1,0:T(8,128)(2,1)S(1)}, bf16[1,264,2048]{2,1,0:T(8,128)(2,1)S(1)}, u32[]{:S(2)}, u32[]{:S(2)}) collective-permute-start(bf16[1,264,2048]{2,1,0:T(8,128)(2,1)S(1)} %collective-permute-done.7), channel_id=1, source_target_pairs={{0,30},{2,0},{4,2},{6,4},{8,6},{10,8},{12,10},{14,12},{16,14},{18,... | collective-permute-start | bytes 3244040 | tf_op jit(solution)/shard_map/ppermute | solution.py:26
  228.6 47.7 %collective-permute-start.10 = (bf16[1,264,2048]{2,1,0:T(8,128)(2,1)S(1)}, bf16[1,264,2048]{2,1,0:T(8,128)(2,1)S(1)}, u32[]{:S(2)}, u32[]{:S(2)}) collective-permute-start(bf16[1,264,2048]{2,1,0:T(8,128)(2,1)S(1)} %collective-permute-done.8), channel_id=1, source_target_pairs={{0,2},{2,4},{4,6},{6,8},{8,10},{10,12},{12,14},{14,16},{16,18},{18... | collective-permute-start | bytes 3244040 | tf_op jit(solution)/shard_map/ppermute | solution.py:21
  250.1 47.5 %collective-permute-start.11 = (bf16[1,264,2048]{2,1,0:T(8,128)(2,1)S(1)}, bf16[1,264,2048]{2,1,0:T(8,128)(2,1)S(1)}, u32[]{:S(2)}, u32[]{:S(2)}) collective-permute-start(bf16[1,264,2048]{2,1,0:T(8,128)(2,1)S(1)} %collective-permute-done.9), channel_id=1, source_target_pairs={{0,30},{2,0},{4,2},{6,4},{8,6},{10,8},{12,10},{14,12},{16,14},{18,... | collective-permute-start | bytes 3244040 | tf_op jit(solution)/shard_map/ppermute | solution.py:26
  276.3 48.1 %collective-permute-start.12 = (bf16[1,264,2048]{2,1,0:T(8,128)(2,1)S(1)}, bf16[1,264,2048]{2,1,0:T(8,128)(2,1)S(1)}, u32[]{:S(2)}, u32[]{:S(2)}) collective-permute-start(bf16[1,264,2048]{2,1,0:T(8,128)(2,1)S(1)} %collective-permute-done.10), channel_id=1, source_target_pairs={{0,2},{2,4},{4,6},{6,8},{8,10},{10,12},{12,14},{14,16},{16,18},{18... | collective-permute-start | bytes 3244040 | tf_op jit(solution)/shard_map/ppermute | solution.py:21
  297.6 47.2 %collective-permute-start.13 = (bf16[1,264,2048]{2,1,0:T(8,128)(2,1)S(1)}, bf16[1,264,2048]{2,1,0:T(8,128)(2,1)S(1)}, u32[]{:S(2)}, u32[]{:S(2)}) collective-permute-start(bf16[1,264,2048]{2,1,0:T(8,128)(2,1)S(1)} %collective-permute-done.11), channel_id=1, source_target_pairs={{0,30},{2,0},{4,2},{6,4},{8,6},{10,8},{12,10},{14,12},{16,14},{18,... | collective-permute-start | bytes 3244040 | tf_op jit(solution)/shard_map/ppermute | solution.py:26
  324.3 44.4 %copy-start.1 = (bf16[1,256,4224]{1,2,0:T(8,128)(2,1)S(1)}, bf16[1,256,4224]{1,2,0:T(8,128)(2,1)}, u32[]{:S(2)}) copy-start(bf16[1,256,4224]{1,2,0:T(8,128)(2,1)} %copy.11) | copy-start | bytes 6488068
  324.3 44.4 %copy-start.2 = (bf16[1,256,4224]{1,2,0:T(8,128)(2,1)S(1)}, bf16[1,256,4224]{1,2,0:T(8,128)(2,1)}, u32[]{:S(2)}) copy-start(bf16[1,256,4224]{1,2,0:T(8,128)(2,1)} %copy.12) | copy-start | bytes 6488068
  324.3 43.3 %collective-permute-start.14 = (bf16[1,264,2048]{2,1,0:T(8,128)(2,1)S(1)}, bf16[1,264,2048]{2,1,0:T(8,128)(2,1)S(1)}, u32[]{:S(2)}, u32[]{:S(2)}) collective-permute-start(bf16[1,264,2048]{2,1,0:T(8,128)(2,1)S(1)} %collective-permute-done.12), channel_id=1, source_target_pairs={{0,2},{2,4},{4,6},{6,8},{8,10},{10,12},{12,14},{14,16},{16,18},{18... | collective-permute-start | bytes 3244040 | tf_op jit(solution)/shard_map/ppermute | solution.py:21
  378.1 10.3 %copy-start.7 = (u32[32]{0:T(128)S(1)}, u32[32]{0:T(128)}, u32[]{:S(2)}) copy-start(u32[32]{0:T(128)} %constant.144) | copy-start | bytes 388
Sparse Core Ops, SparseCore 0:
  388.5 10.8 reduce-scatter.1
